TPU v7x, 32 devices: a whole 2x2x4 slice. The times are simulated.
32 devices in a mesh: lat: 8 (over z, core), ch: 4 (over y, x).
Axes of the slice: x: 2, y: 2, z: 4, core: 2. Of those that a mesh axis runs over, the one named last changes fastest.
Arguments:
- fields: bfloat16 [2, 704, 32, 1440], P(None, 'lat', 'ch'), may hold values from -6 to 6
- table: bfloat16 [704, 704, 352], P('lat', 'ch'), may hold values from -1 to 1, as said below
Outputs:
- coefficients: float32 [704, 704, 128], P('lat', 'ch')
Inputs may be any that keep to these rules, and one draw needn't show every extreme that they name: table[m, l, k] is zero wherever l < m.
All inputs are finite; a program needn't handle non-finite values.
Results may differ from a plain program's by a relative error of at most 0.005.
Values may be sent and summed in bfloat16 or wider, within the bound.
No kernel may reach another device: no remote copies, remote signals or barrier semaphores. Data moves between devices by JAX's collectives and lax.ppermute only.
A program may use at most 128 MiB of HBM per device.

v0:
```python
import math

import jax
import jax.numpy as jnp
from jax import lax
from jax.sharding import PartitionSpec as P

MODES = 704


def fourier_table(nlon, modes):
    cols = jnp.arange(nlon, dtype=jnp.int32)[:, None]
    orders = jnp.arange(modes, dtype=jnp.int32)[None, :]
    phase = (cols * orders % nlon).astype(jnp.float32) * (2.0 * math.pi / nlon)
    factor = 1.0 / math.sqrt(nlon)
    return jnp.concatenate([jnp.cos(phase) * factor, -jnp.sin(phase) * factor], axis=1).astype(
        jnp.bfloat16
    )


def parity_project(block, parts, order_start, degree_start):
    order_count, degree_count, hemisphere = block.shape
    padding = degree_count % 2
    first_rows = block[:, 0::2]
    second_rows = block[:, 1::2]
    orders = order_start + jnp.arange(order_count, dtype=jnp.int32)[:, None, None]
    aligned = (degree_start - orders) % 2 == 0
    sym_table = jnp.where(aligned, first_rows, second_rows)
    anti_table = jnp.where(aligned, second_rows, first_rows)
    sym_coeffs = jnp.einsum(
        "mlk,bkcrm->mlbcr", sym_table, parts[:, :hemisphere], preferred_element_type=jnp.float32
    )
    anti_coeffs = jnp.einsum(
        "mlk,bkcrm->mlbcr", anti_table, parts[:, hemisphere:], preferred_element_type=jnp.float32
    )
    chosen = aligned[:, :, :, None, None]
    first_out = jnp.where(chosen, sym_coeffs, anti_coeffs)
    second_out = jnp.where(chosen, anti_coeffs, sym_coeffs)
    joined = jnp.stack([first_out, second_out], axis=2)
    joined = joined.reshape((order_count, degree_count + padding) + sym_coeffs.shape[2:])
    return joined


def shards(fields, table):
    batch, rows, chans, nlon = fields.shape
    slab, lblock, half = table.shape
    fourier = fourier_table(nlon, MODES)
    spectrum = jnp.einsum("brcj,jn->brcn", fields, fourier, preferred_element_type=jnp.float32)
    spectrum = spectrum.astype(jnp.bfloat16).reshape(batch, rows, chans, 2, MODES)
    moved = lax.all_to_all(spectrum, "lat", split_axis=4, concat_axis=1, tiled=True)
    north = moved[:, :half].astype(jnp.float32)
    south = moved[:, half:][:, ::-1].astype(jnp.float32)
    parts = jnp.concatenate(
        [(north + south).astype(jnp.bfloat16), (north - south).astype(jnp.bfloat16)], axis=1
    )
    order_start = lax.axis_index("lat") * slab
    degree_start = lax.axis_index("ch") * lblock
    gathered = parity_project(
        table, lax.all_gather(parts, "ch", axis=2, tiled=True), order_start, degree_start
    )
    return gathered.reshape(slab, lblock, -1)


def solution(mesh):
    return jax.shard_map(
        shards,
        mesh=mesh,
        in_specs=(P(None, "lat", "ch", None), P("lat", "ch", None)),
        out_specs=P("lat", "ch", None),
        check_vma=False,
    )
```

profile of v0, /device:TPU:8, one launch (start us, length us, event | category | flops | bytes accessed | tf_op | source)
XLA Modules:
  0.0 463.8 jit_solution(3976556673803622666)
XLA Ops:
  6.5 0.0 all-gather.2.cloned.1.call-start
  6.5 0.0 copy-start
  6.5 19.1 %multiply_convert_fusion = (bf16[1440,704]{1,0:T(8,128)(2,1)S(1)}, bf16[1440,704]{1,0:T(8,128)(2,1)S(1)}) fusion(), kind=kLoop, calls=%fused_computation.19 | loop fusion | flops 14192640 | bytes 4055040 | tf_op jit(solution)/shard_map/convert.1
  25.7 0.0 copy-done
  25.7 9.1 %fusion.20 = bf16[2,88,8,1408]{3,1,2,0:T(8,128)(2,1)} fusion(bf16[2,88,8,1440]{3,2,1,0:T(8,128)(2,1)S(1)} %copy-done, bf16[1440,704]{1,0:T(8,128)(2,1)S(1)} %get-tuple-element.9, bf16[1440,704]{1,0:T(8,128)(2,1)S(1)} %get-tuple-element.10), kind=kOutput, calls=%fused_computation.33 | convolution fusion | flops 5719588864 | bytes 12075008 | tf_op jit(solution)/shard_map/brcj,jn->brcn/dot_general | solution.py:48
  34.7 10.7 %reshape.46 = bf16[2,88,8,2,704]{4,3,1,2,0:T(2,128)(2,1)} reshape(bf16[2,88,8,1408]{3,1,2,0:T(8,128)(2,1)} %fusion.20) | data formatting | bytes 7929856 | tf_op jit(solution)/shard_map/reshape | solution.py:49
  45.5 11.1 %copy.15 = bf16[2,88,8,2,704]{1,2,3,0,4:T(8,128)(2,1)} copy(bf16[2,88,8,2,704]{4,3,1,2,0:T(2,128)(2,1)} %reshape.46) | data formatting | bytes 7929856 | tf_op jit(solution)/shard_map/reshape | solution.py:49
  56.5 130.8 %all_to_all.18 = bf16[2,88,8,2,704]{1,2,3,0,4:T(8,128)(2,1)S(1)} all-to-all(bf16[2,88,8,2,704]{1,2,3,0,4:T(8,128)(2,1)} %copy.15), channel_id=1, replica_groups=mesh['lat'=8,'ch'=4] {'lat'}, dimensions={4} | all-to-all | bytes 7929856 | tf_op jit(solution)/shard_map/all_to_all | solution.py:50
  187.3 9.2 %copy.27 = bf16[2,88,8,2,8,88]{1,4,2,3,0,5:T(8,128)(2,1)} copy(bf16[2,88,8,2,8,88]{1,2,3,0,5,4:T(8,128)(2,1)S(1)} %bitcast.42) | data formatting | bytes 7929856 | tf_op jit(solution)/shard_map/all_to_all | solution.py:50
  196.5 9.7 %all_to_all.16 = bf16[2,704,8,2,88]{1,2,3,0,4:T(8,128)(2,1)} reshape(bf16[2,8,88,8,2,88]{2,1,3,4,0,5:T(8,128)(2,1)} %bitcast.43) | data formatting | bytes 7929856 | tf_op jit(solution)/shard_map/all_to_all | solution.py:50
  206.1 4.3 slice.25
  210.5 0.0 slice-start
  210.5 6.9 %reverse = bf16[2,384,8,2,88]{1,2,3,0,4:T(8,128)(2,1)S(1)} reverse(bf16[2,384,8,2,88]{1,2,3,0,4:T(8,128)(2,1)} %bitcast.44), dimensions={1} | reverse | bytes 4325376
  217.4 0.0 slice-start.1
  217.4 3.5 fusion.15
  220.9 0.0 slice-done
  221.0 0.0 slice-done.1
  221.0 0.7 fusion.16
  221.6 3.9 pad_maximum_fusion.1
  225.5 0.0 all-gather.2.cloned.1.call-update
  225.5 48.5 %slice.19 = bf16[88,88,352]{2,1,0:T(8,128)(2,1)} slice(bf16[88,176,352]{2,1,0:T(8,128)(2,1)} %param.3), slice={[0:88:1], [1:176:2], [0:352:1]} | slice | bytes 10903552 | tf_op jit(solution)/shard_map/slice | solution.py:25
  274.1 48.4 %slice.18 = bf16[88,88,352]{2,1,0:T(8,128)(2,1)} slice(bf16[88,176,352]{2,1,0:T(8,128)(2,1)} %param.3), slice={[0:88:1], [0:176:2], [0:352:1]} | slice | bytes 10903552 | tf_op jit(solution)/shard_map/slice | solution.py:24
  322.5 66.9 %all-gather.2.cloned.1.call-done = bf16[2,704,32,2,88]{1,2,3,0,4:T(8,128)(2,1)} async-done(((bf16[2,704,8,2,88]{1,2,3,0,4:T(8,128)(2,1)}), bf16[2,704,32,2,88]{1,2,3,0,4:T(8,128)(2,1)}) %all-gather.2.cloned.1.call-update) | async-done | bytes 15859728 | tf_op jit(solution)/shard_map/all_gather | solution.py:59
  389.3 14.1 %fusion = f32[88,88,2,32,2]{1,3,4,2,0:T(8,128)} fusion(bf16[2,704,32,2,88]{1,2,3,0,4:T(8,128)(2,1)} %all-gather.2.cloned.1.call-done, bf16[88,88,352]{2,1,0:T(8,128)(2,1)} %slice.19, bf16[88,88,352]{2,1,0:T(8,128)(2,1)} %slice.18, pred[88]{0:T(512)(128)(4,1)S(1)} %fusion.23), kind=kOutput, calls=%fused_computation.1 | convolution fusion | flops 700553216 | bytes 24510552 | tf_op jit(solution)/shard_map/mlk,bkcrm->mlbcr/dot_general | solution.py:33
  403.4 14.6 %select_bitcast_fusion.1 = (f32[88,88,1,2,32,2]{1,4,5,3,0,2:T(8,128)}, f32[88,88,1,2,32,2]{1,4,5,3,0,2:T(8,128)}) fusion(f32[88,88,2,32,2]{1,3,4,2,0:T(8,128)} %fusion, pred[88]{0:T(512)(128)(4,1)S(1)} %fusion.23, bf16[2,704,32,2,88]{1,2,3,0,4:T(8,128)(2,1)} %all-gather.2.cloned.1.call-done, bf16[88,88,352]{2,1,0:T(8,128)(2,1)} %slice.18, ...), kind=kOutput, calls=%fused_computation.14 | convolution fusion | flops 702535680 | bytes 34243584 | tf_op jit(solution)/shard_map/mlk,bkcrm->mlbcr/dot_general | solution.py:30
  417.9 11.5 %pad_maximum_fusion = f32[88,88,2,2,32,2]{1,4,5,3,0,2:T(8,128)} fusion(f32[88,88,1,2,32,2]{1,4,5,3,0,2:T(8,128)} %get-tuple-element.8, f32[88,88,1,2,32,2]{1,4,5,3,0,2:T(8,128)} %get-tuple-element.7), kind=kLoop, calls=%fused_computation | loop fusion | flops 1982464 | bytes 15859712 | tf_op jit(solution)/shard_map/stack | solution.py:39
  429.4 16.4 %copy.17 = f32[88,88,2,2,32,2]{0,5,4,3,2,1:T(2,128)} copy(f32[88,88,2,2,32,2]{1,4,5,3,0,2:T(8,128)} %pad_maximum_fusion) | data formatting | bytes 15859712 | tf_op jit(solution)/shard_map/stack | solution.py:39
  445.8 11.1 %copy.18 = f32[88,176,128]{2,1,0:T(8,128)} copy(f32[88,176,128]{0,2,1:T(8,128)} %bitcast.39) | data formatting | bytes 15859712 | tf_op jit(solution)/shard_map/reshape;reshape | solution.py:61
  (2 shorter events, 0.0 us)
Async XLA Ops:
  6.5 382.8 %all-gather.2.cloned.1.call-start = ((), (), s32[]{:S(2)}) async-start(), calls=%async_computation.1 | async-start | bytes 21626880 | tf_op jit(solution)/shard_map/all_gather | solution.py:59
  6.5 19.1 %copy-start = (bf16[2,88,8,1440]{3,2,1,0:T(8,128)(2,1)S(1)}, bf16[2,88,8,1440]{3,2,1,0:T(8,128)(2,1)}, u32[]{:S(2)}) copy-start(bf16[2,88,8,1440]{3,2,1,0:T(8,128)(2,1)} %param.2) | copy-start | bytes 12165124
  210.5 10.5 %slice-start = ((s8[4325376]{0:T(1024)(128)(4,1)}), s8[131072]{0:T(1024)(128)(4,1)S(1)}, s32[]{:S(2)}) async-start(s8[4325376]{0:T(1024)(128)(4,1)} %bitcast.40), calls=%async_computation.2 | async-start | bytes 262144
  217.4 3.5 slice-start.1
Sparse Core Ops, SparseCore 0:
  225.7 163.6 all-gather.1
where the time goes:
time: 469 us; the launch traced here: 464 us
  local copies, waits for them, and re-layouts  176 us (38%)
  blocking collectives  131 us (28%)
  waiting for transfers between devices  66.9 us (14%)
  other arithmetic  38.6 us (8%)
  matrix products  37.7 us (8%)
  between operations  13.5 us (3%)
    all_to_all x1, blocking collectives, shards(): lax.all_to_all(spectrum, 'lat', split_axis=4, concat_axis=1, tiled=True)  131 us
    all_gather x1, waiting for transfers between devices, shards(): lax.all_gather(parts, 'ch', axis=2, tiled=True)  66.9 us
    slice x1, local copies, waits for them, and re-layouts, parity_project(): second_rows = block[:, 1::2]  48.5 us
    slice x1, local copies, waits for them, and re-layouts, parity_project(): first_rows = block[:, 0::2]  48.4 us
    reshape x2, local copies, waits for them, and re-layouts, shards(): spectrum.astype(jnp.bfloat16).reshape(batch, rows, chans, 2, MODES)  21.8 us
    another operation x1, other arithmetic  19.1 us
    all_to_all x2, local copies, waits for them, and re-layouts, shards(): lax.all_to_all(spectrum, 'lat', split_axis=4, concat_axis=1, tiled=True)  18.9 us
    another operation x1, local copies, waits for them, and re-layouts, parity_project(): joined = jnp.stack([first_out, second_out], axis=2)  16.4 us
  transfers between devices with their start and end apart: 1, of which 1 were waited for; matrix products, arithmetic and copies ran while one was open for 21% of the time, Pallas kernels for 0%

commit v1 on v0

v1 whole, which is shorter than its diff:
```python
import functools
import math

import jax
import jax.numpy as jnp
import ml_dtypes
import numpy as np
from jax import lax
from jax.experimental import pallas as pl
from jax.experimental.pallas import tpu as pltpu
from jax.sharding import PartitionSpec as P

LANES = 128
VMEM_LIMIT = 56 * 1024 * 1024
NT = (((1,), (1,)), ((), ()))


def fourier_rows(nlon, slabs, slab, chunk):
    first, count = chunk
    orders = (np.arange(slabs)[:, None] * slab + first + np.arange(count)[None, :]).astype(np.int32)
    cols = np.arange(nlon, dtype=np.int32)
    phase = (orders[:, :, None] * cols % nlon).astype(np.float32) * np.float32(2.0 * math.pi / nlon)
    factor = np.float32(1.0 / math.sqrt(nlon))
    rows = np.stack([np.cos(phase) * factor, -np.sin(phase) * factor], axis=1)
    return rows.astype(np.float32).astype(ml_dtypes.bfloat16).reshape(slabs, 2 * count, nlon)


def reorder_matrices(rows, chans):
    out = np.zeros((2, chans, rows, rows, chans), np.float32)
    for c in range(chans):
        for k in range(rows):
            out[0, c, k, k, c] = 1
            out[1, c, k, rows - 1 - k, c] = 1
    return out.reshape(2, chans * rows, rows * chans).astype(ml_dtypes.bfloat16)


def split_orders(slab):
    if slab % 8:
        return [(0, slab)]
    units = slab // 8
    parts = min(4, units)
    sizes = [(units * (p + 1) // parts - units * p // parts) * 8 for p in range(parts)]
    starts = np.cumsum([0] + sizes)
    return [(int(s), int(n)) for s, n in zip(starts, sizes)]


def xor_pairs(size, step):
    return [(i, i ^ step) for i in range(size)]


def reorder_kernel(south_ref, pick_ref, fields_ref, out_ref):
    out_ref[0] = jnp.dot(pick_ref[0], fields_ref[0], preferred_element_type=jnp.float32).astype(out_ref.dtype)


def reorder(fields, south):
    batch, rows, chans, nlon = fields.shape
    flat = rows * chans
    picks = jnp.asarray(reorder_matrices(rows, chans))
    out = pl.pallas_call(
        reorder_kernel,
        grid_spec=pltpu.PrefetchScalarGridSpec(
            num_scalar_prefetch=1,
            grid=(batch,),
            in_specs=[
                pl.BlockSpec((1, flat, flat), lambda b, south: (south[0], 0, 0)),
                pl.BlockSpec((1, flat, nlon), lambda b, south: (b, 0, 0)),
            ],
            out_specs=pl.BlockSpec((1, flat, nlon), lambda b, south: (b, 0, 0)),
        ),
        out_shape=jax.ShapeDtypeStruct((batch, flat, nlon), fields.dtype),
        compiler_params=pltpu.CompilerParams(vmem_limit_bytes=VMEM_LIMIT),
        name="reorder",
    )(south, picks, fields.reshape(batch, flat, nlon))
    return out.reshape(batch * flat, nlon)


def dft_kernel(slabs, me_ref, rows_ref, fields_ref, *refs):
    outs, lhs = refs[:slabs], refs[slabs]
    me = me_ref[0]
    count, nlon = rows_ref.shape[1:]
    width = fields_ref.shape[0]
    joined = count % 16 == 0
    for d in range(slabs):
        lhs[d] = rows_ref[me ^ d]
    for n0 in range(0, width, 256):
        cols = slice(n0, min(n0 + 256, width))
        block = fields_ref[cols, :]
        if joined:
            res = lax.dot_general(
                lhs[...].reshape(slabs * count, nlon), block, NT, preferred_element_type=jnp.float32
            )
            for d in range(slabs):
                outs[d][:, cols] = res[d * count : (d + 1) * count].astype(jnp.bfloat16)
        else:
            for d in range(slabs):
                res = lax.dot_general(lhs[d], block, NT, preferred_element_type=jnp.float32)
                outs[d][:, cols] = res.astype(jnp.bfloat16)


def dft(flat, rows, me):
    slabs, count, nlon = rows.shape
    width = flat.shape[0]
    vmem = pl.BlockSpec(memory_space=pltpu.VMEM)
    return pl.pallas_call(
        functools.partial(dft_kernel, slabs),
        in_specs=[pl.BlockSpec(memory_space=pltpu.SMEM), vmem, vmem],
        out_specs=[vmem] * slabs,
        out_shape=[jax.ShapeDtypeStruct((count, width), jnp.bfloat16)] * slabs,
        scratch_shapes=[pltpu.VMEM((slabs, count, nlon), jnp.bfloat16)],
        compiler_params=pltpu.CompilerParams(vmem_limit_bytes=VMEM_LIMIT),
        cost_estimate=pl.CostEstimate(
            flops=2 * slabs * count * nlon * width,
            bytes_accessed=2 * (slabs * count * (nlon + width) + width * nlon),
            transcendentals=0,
        ),
        name="dft",
    )(me, jnp.asarray(rows), flat)


def packs(names, depth):
    return names % 64 == 0 and depth % LANES == 96


def packed_rows(names, depth):
    tiles = -(-depth // LANES)
    return names * depth // LANES if packs(names, depth) else names * tiles


def parity_kernel(slabs, batch, chans, band, me_ref, *refs):
    xs, out_ref, held = refs[:slabs], refs[slabs], refs[slabs + 1]
    turned = refs[slabs + 2 :]
    me = me_ref[0]
    count = xs[0].shape[0] // 2
    names = 4 * batch * chans
    depth = band * slabs // 2
    for d in range(slabs):
        held[me ^ d] = xs[d][...].astype(jnp.float32)
    for i in range(slabs // 2):
        north, south = held[i], held[slabs - 1 - i]
        held[i] = north + south
        held[slabs - 1 - i] = north - south
    for r in range(2):
        orders = slice(r * count, (r + 1) * count)
        for bc in range(batch * chans):
            lanes = slice(bc * band, (bc + 1) * band)
            for s in range(2):
                bands = [i if s == 0 else slabs - 1 - i for i in range(slabs // 2)]
                line = jnp.concatenate([held[i, orders, lanes] for i in bands], axis=1)
                name = (s * batch * chans + bc) * 2 + r
                for t, tile in enumerate(turned):
                    piece = line[:, t * LANES : min((t + 1) * LANES, depth)]
                    if piece.shape[1] < LANES:
                        blank = jnp.zeros((count, LANES - piece.shape[1]), jnp.float32)
                        piece = jnp.concatenate([piece, blank], axis=1)
                    tile[pl.ds(name, count, stride=names), :] = piece
    packed = packs(names, depth)

    def write(m, carry):
        rows = pl.ds(pl.multiple_of(m * names, names), names)
        for t, tile in enumerate(turned):
            block = tile[rows, :].astype(jnp.bfloat16)
            if packed and t == len(turned) - 1:
                step = names // 4
                last = block[3 * step :]
                for g in range(3):
                    both = jnp.concatenate(
                        [block[g * step : (g + 1) * step, :96], last[:, 32 * g : 32 * (g + 1)]], axis=1
                    )
                    out_ref[m, t * names + g * step : t * names + (g + 1) * step, :] = both
            else:
                out_ref[m, t * names : (t + 1) * names, :] = block
        return carry

    lax.fori_loop(0, count, write, 0)


def parity(blocks, me, batch, chans, band):
    slabs = len(blocks)
    count = blocks[0].shape[0] // 2
    width = blocks[0].shape[1]
    names = 4 * batch * chans
    depth = band * slabs // 2
    vmem = pl.BlockSpec(memory_space=pltpu.VMEM)
    total = packed_rows(names, depth)
    return pl.pallas_call(
        functools.partial(parity_kernel, slabs, batch, chans, band),
        in_specs=[pl.BlockSpec(memory_space=pltpu.SMEM)] + [vmem] * slabs,
        out_specs=vmem,
        out_shape=jax.ShapeDtypeStruct((count, total, LANES), jnp.bfloat16),
        scratch_shapes=[pltpu.VMEM((slabs, 2 * count, width), jnp.float32)]
        + [pltpu.VMEM((count * names, LANES), jnp.float32)] * -(-depth // LANES),
        compiler_params=pltpu.CompilerParams(vmem_limit_bytes=VMEM_LIMIT),
        cost_estimate=pl.CostEstimate(
            flops=40 * slabs * count * width, bytes_accessed=8 * slabs * count * width, transcendentals=0
        ),
        name="parity",
    )(me, *blocks)


def project_kernel(groups, batch, first, info_ref, table_ref, *refs):
    parts, out_ref, rhs = refs[:groups], refs[-2], refs[-1]
    me, odd = info_ref[0], info_ref[1]
    orders, degrees, depth = table_ref.shape
    inner = rhs.shape[3]
    names = 2 * batch * inner
    packed = packs(names, depth)
    tiles = -(-depth // LANES)
    for m in range(orders):
        for d in range(groups):
            ch = me ^ d
            for sb in range(2 * batch):
                for t in range(tiles):
                    width = min(LANES, depth - t * LANES)
                    base = t * names
                    if packed and t == tiles - 1:
                        step = names // 4
                        if (sb + 1) * inner <= 3 * step:
                            block = parts[d][m, base + sb * inner : base + (sb + 1) * inner, :width]
                        else:
                            off = sb * inner - 3 * step
                            block = jnp.concatenate(
                                [
                                    parts[d][m, base + g * step + off : base + g * step + off + inner, 96:]
                                    for g in range(3)
                                ],
                                axis=1,
                            )
                    else:
                        block = parts[d][m, base + sb * inner : base + (sb + 1) * inner, :width]
                    rhs[m, sb, ch, :, t * LANES : t * LANES + width] = block
    row = lax.broadcasted_iota(jnp.int32, (degrees, batch * groups * inner), 0)
    start = pl.program_id(0) * orders + first
    for m in range(orders):
        right = rhs[m].reshape(2 * batch * groups * inner, depth)
        both = lax.dot_general(table_ref[m], right, NT, preferred_element_type=jnp.float32)
        cut = batch * groups * inner
        even = ((row + (odd + start + m)) & 1) == 0
        out_ref[m] = jnp.where(even, both[:, :cut], both[:, cut:])


def project(table, parts, info, first, batch, inner, prior):
    slab, degrees, depth = table.shape
    groups = len(parts)
    count, total, _ = parts[0].shape
    step = 8 if count % 8 == 0 else count
    lead = first // step
    names = batch * groups * inner
    operands = [info, table, *parts]
    in_specs = [
        pl.BlockSpec(memory_space=pltpu.SMEM),
        pl.BlockSpec((step, degrees, depth), lambda g: (g + lead, 0, 0)),
    ] + [pl.BlockSpec((step, total, LANES), lambda g: (g, 0, 0))] * groups
    aliases = {}
    if prior is not None:
        operands.append(prior)
        in_specs.append(pl.BlockSpec(memory_space=pl.ANY))
        aliases = {len(operands) - 1: 0}
    return pl.pallas_call(
        functools.partial(project_kernel, groups, batch, first),
        grid=(count // step,),
        in_specs=in_specs,
        out_specs=pl.BlockSpec((step, degrees, names), lambda g: (g + lead, 0, 0)),
        out_shape=jax.ShapeDtypeStruct((slab, degrees, names), jnp.float32),
        scratch_shapes=[pltpu.VMEM((step, 2 * batch, groups, inner, depth), jnp.bfloat16)],
        input_output_aliases=aliases,
        compiler_params=pltpu.CompilerParams(vmem_limit_bytes=VMEM_LIMIT),
        cost_estimate=pl.CostEstimate(
            flops=4 * count * degrees * depth * names,
            bytes_accessed=count * degrees * (2 * depth + 4 * names) + 2 * groups * count * total * LANES,
            transcendentals=0,
        ),
        name="project",
    )(*operands)


def shards(slabs, groups, fields, table):
    batch, band, chans, nlon = fields.shape
    slab, degrees, depth = table.shape
    lat, ch = lax.axis_index("lat"), lax.axis_index("ch")
    me = lat.astype(jnp.int32).reshape(1)
    south = (me >= slabs // 2).astype(jnp.int32)
    odd = (ch * degrees + lat * slab) % 2
    info = jnp.stack([ch, odd]).astype(jnp.int32)
    flat = reorder(fields, south)
    chunks = split_orders(slab)
    out = None
    for q, (first, count) in enumerate(chunks):
        sends = dft(flat, fourier_rows(nlon, slabs, slab, (first, count)), me)
        blocks = [sends[0]] + [
            lax.ppermute(sends[d], "lat", xor_pairs(slabs, d)) for d in range(1, slabs)
        ]
        mine = parity(blocks, me, batch, chans, band)
        bits = [1 << k for k in range(groups.bit_length() - 1)]
        if q % 2:
            bits = bits[::-1]
        parts = {0: mine}
        for bit in bits:
            parts.update({d ^ bit: lax.ppermute(parts[d], "ch", xor_pairs(groups, bit)) for d in list(parts)})
        out = project(table, [parts[d] for d in range(groups)], info, first, batch, 2 * chans, out)
    return out


def solution(mesh):
    return jax.shard_map(
        functools.partial(shards, mesh.shape["lat"], mesh.shape["ch"]),
        mesh=mesh,
        in_specs=(P(None, "lat", "ch", None), P("lat", "ch", None)),
        out_specs=P("lat", "ch", None),
        check_vma=False,
    )
```

time: 469 us -> 242 us (0.52)
  local copies, waits for them, and re-layouts: 176 us -> 1.5 us
  blocking collectives: 131 us -> 0 us
  Pallas kernels: 0 us -> 78.3 us
  waiting for transfers between devices: 66.9 us -> 117 us
  starting transfers between devices: 0.01 us -> 40.4 us
  other arithmetic: 38.6 us -> 0.66 us
  matrix products: 37.7 us -> 0 us
  between operations: 13.5 us -> 0.41 us
    all_to_all x1 -> x0, blocking collectives: 131 us -> none  [shards(): lax.all_to_all(spectrum, 'lat', split_axis=4, concat_axis=1, tiled=True)]
    ppermute x0 -> x40, waiting for transfers between devices: none -> 117 us  [the longest x12 82.8 us: shards(): lax.ppermute(parts[d], 'ch', xor_pairs(groups, bit))]
    slice x3 -> x0, local copies, waits for them, and re-layouts: 101 us -> none  [the longest x1 48.5 us: parity_project(): second_rows = block[:, 1::2]]
    pallas_call x0 -> x13, Pallas kernels: none -> 78.3 us  [the longest x4 26.1 us: parity(): pl.pallas_call(functools.partial(parity_kernel, slabs, batch, chans, band...]
    all_gather x1 -> x0, waiting for transfers between devices: 66.9 us -> none  [shards(): lax.all_gather(parts, 'ch', axis=2, tiled=True)]
    ppermute x0 -> x40, starting transfers between devices: none -> 40.4 us  [the longest x28 26 us: shards(): lax.ppermute(sends[d], 'lat', xor_pairs(slabs, d))]
    dot_general x3 -> x0, matrix products: 37.7 us -> none  [the longest x1 14.6 us: parity_project(): jnp.einsum('mlk,bkcrm->mlbcr', sym_table, parts[:, :hemisphere], preferre...]
    another operation x2 -> x1, other arithmetic: 30.6 us -> 0.66 us  [shards(): info = jnp.stack([ch, odd]).astype(jnp.int32)]
  transfers between devices with their start and end apart: 1 -> 40, of which waited for: 1 -> 19; matrix products, arithmetic and copies ran while one was open for 21% -> 0% of each run, Pallas kernels for 0% -> 25%
where the time goes in v1:
time: 242 us; the launch traced here: 239 us
  waiting for transfers between devices  117 us (48%)
  Pallas kernels  78.3 us (32%)
  starting transfers between devices  40.4 us (17%)
    ppermute x12, waiting for transfers between devices, shards(): lax.ppermute(parts[d], 'ch', xor_pairs(groups, bit))  82.8 us
    ppermute x28, waiting for transfers between devices, shards(): lax.ppermute(sends[d], 'lat', xor_pairs(slabs, d))  34.4 us
    pallas_call x4, Pallas kernels, parity(): pl.pallas_call(functools.partial(parity_kernel, slabs, batch, chans, band...  26.1 us
    ppermute x28, starting transfers between devices, shards(): lax.ppermute(sends[d], 'lat', xor_pairs(slabs, d))  26 us
    pallas_call x4, Pallas kernels, project(): pl.pallas_call(functools.partial(project_kernel, groups, batch, first), g...  24 us
    pallas_call x4, Pallas kernels, dft(): pl.pallas_call(functools.partial(dft_kernel, slabs), in_specs=[pl.BlockSp...  21.4 us
    ppermute x12, starting transfers between devices, shards(): lax.ppermute(parts[d], 'ch', xor_pairs(groups, bit))  14.4 us
    pallas_call x1, Pallas kernels, reorder(): pl.pallas_call(reorder_kernel, grid_spec=pltpu.PrefetchScalarGridSpec(num...  6.93 us
  transfers between devices with their start and end apart: 40, of which 19 were waited for; matrix products, arithmetic and copies ran while one was open for 0% of the time, Pallas kernels for 25%

profile of v1, /device:TPU:8, one launch (start us, length us, event | category | flops | bytes accessed | tf_op | source)
XLA Modules:
  0.0 238.5 jit_solution(6916220366194028183)
XLA Ops:
  0.0 6.9 %reorder.1 = bf16[2,704,1440]{2,1,0:T(8,128)(2,1)} custom-call(s32[1]{0:T(128)S(6)} %convert_element_type.3.south_ref, bf16[2,704,704]{2,1,0:T(8,128)(2,1)} %constant.38.clone.pick_ref, bf16[2,704,1440]{2,1,0:T(8,128)(2,1)} %bitcast.9), custom_call_target="tpu_custom_call" | custom-call | tf_op jit(solution)/shard_map/reorder/pallas_call | solution.py:59
  6.9 4.7 %dft.7 = (bf16[32,1408]{1,0:T(8,128)(2,1)}, bf16[32,1408]{1,0:T(8,128)(2,1)}, bf16[32,1408]{1,0:T(8,128)(2,1)}, bf16[32,1408]{1,0:T(8,128)(2,1)}, bf16[32,1408]{...) custom-call(s32[1]{0:T(128)} %bitcast.2.me_ref, ...), custom_call_target="tpu_custom_call" | custom-call | flops 1038090240 | bytes 5513216 | tf_op jit(solution)/shard_map/dft/pallas_call | solution.py:104
  11.7 1.8 collective-permute-start.32
  13.5 2.6 %collective-permute-start.33 = (bf16[32,1408]{1,0:T(8,128)(2,1)}, bf16[32,1408]{1,0:T(8,128)(2,1)S(1)}, u32[]{:S(2)}, u32[]{:S(2)}) collective-permute-start(bf16[32,1408]{1,0:T(8,128)(2,1)} %get-tuple-element.65), channel_id=1, source_target_pairs={{0,16},{4,20},{8,24},{12,28},{16,0},{20,4},{24,8},{28,12},{1,17},{... | collective-permute-start | bytes 270344 | tf_op jit(solution)/shard_map/ppermute | solution.py:290
  16.1 1.5 collective-permute-start.35
  17.7 0.3 collective-permute-start.36
  17.9 5.5 %dft.6 = (bf16[48,1408]{1,0:T(8,128)(2,1)}, bf16[48,1408]{1,0:T(8,128)(2,1)}, bf16[48,1408]{1,0:T(8,128)(2,1)}, bf16[48,1408]{1,0:T(8,128)(2,1)}, bf16[48,1408]{...) custom-call(s32[1]{0:T(128)} %bitcast.2.me_ref, ...), custom_call_target="tpu_custom_call" | custom-call | flops 1557135360 | bytes 6242304 | tf_op jit(solution)/shard_map/dft/pallas_call | solution.py:104
  23.5 1.1 collective-permute-start.20
  24.6 2.5 %collective-permute-done.33.refs_4_ = bf16[32,1408]{1,0:T(8,128)(2,1)S(1)} collective-permute-done((bf16[32,1408]{1,0:T(8,128)(2,1)}, bf16[32,1408]{1,0:T(8,128)(2,1)S(1)}, u32[]{:S(2)}, u32[]{:S(2)}) %collective-permute-start.33) | collective-permute-done | bytes 90144 | tf_op jit(solution)/shard_map/ppermute | solution.py:290
  27.1 1.9 collective-permute-done.34.refs_5_
  29.1 0.9 collective-permute-start.22
  29.9 1.0 collective-permute-done.35.refs_6_
  31.0 0.2 collective-permute-start.23
  31.2 1.4 collective-permute-done.36.refs_7_
  32.5 0.5 collective-permute-start.24
  33.0 5.6 %dft.5 = (bf16[48,1408]{1,0:T(8,128)(2,1)}, bf16[48,1408]{1,0:T(8,128)(2,1)}, bf16[48,1408]{1,0:T(8,128)(2,1)}, bf16[48,1408]{1,0:T(8,128)(2,1)}, bf16[48,1408]{...) custom-call(s32[1]{0:T(128)} %bitcast.2.me_ref, ...), custom_call_target="tpu_custom_call" | custom-call | flops 1557135360 | bytes 6242304 | tf_op jit(solution)/shard_map/dft/pallas_call | solution.py:104
  38.7 1.6 collective-permute-start.25
  40.3 1.6 collective-permute-start.26
  42.1 3.5 %collective-permute-start.11 = (bf16[48,1408]{1,0:T(8,128)(2,1)}, bf16[48,1408]{1,0:T(8,128)(2,1)S(1)}, u32[]{:S(2)}, u32[]{:S(2)}) collective-permute-start(bf16[48,1408]{1,0:T(8,128)(2,1)} %get-tuple-element.47), channel_id=1, source_target_pairs={{0,8},{4,12},{8,0},{12,4},{16,24},{20,28},{24,16},{28,20},{1,9},{5... | collective-permute-start | bytes 405512 | tf_op jit(solution)/shard_map/ppermute | solution.py:290
  45.6 5.1 %parity.7.refs_0_ = bf16[16,176,128]{2,1,0:T(8,128)(2,1)} custom-call(s32[1]{0:T(128)} %bitcast.2.me_ref, bf16[32,1408]{1,0:T(8,128)(2,1)} %get-tuple-element.61.refs_0_, bf16[32,1408]{1,0:T(8,128)(2,1)} %copy-done.30, bf16[32,1408]{1,0:T(8,128)(2,1)} %copy-done.31, bf16[32,1408]{1,0:T(8,128)(2,1)} %copy-done.32, bf16[32,1408]{1,0:T(8,128)(2,1)} %copy-done.33, ...), custom_call_target="tpu_custom_call" | custom-call | flops 7208960 | bytes 1441792 | tf_op jit(solution)/shard_map/parity/pallas_call | solution.py:185
  50.7 1.6 collective-permute-start.37
  52.3 1.6 collective-permute-done.25.refs_6_
  53.9 3.0 %collective-permute-done.26.refs_7_ = bf16[48,1408]{1,0:T(8,128)(2,1)S(1)} collective-permute-done((bf16[48,1408]{1,0:T(8,128)(2,1)S(1)}, bf16[48,1408]{1,0:T(8,128)(2,1)S(1)}, u32[]{:S(2)}, u32[]{:S(2)}) %collective-permute-start.26) | collective-permute-done | bytes 135200 | tf_op jit(solution)/shard_map/ppermute | solution.py:290
  56.9 2.3 collective-permute-start.14
  59.2 1.2 collective-permute-start.15
  60.4 5.5 %dft.4 = (bf16[48,1408]{1,0:T(8,128)(2,1)}, bf16[48,1408]{1,0:T(8,128)(2,1)}, bf16[48,1408]{1,0:T(8,128)(2,1)}, bf16[48,1408]{1,0:T(8,128)(2,1)}, bf16[48,1408]{...) custom-call(s32[1]{0:T(128)} %bitcast.2.me_ref, ...), custom_call_target="tpu_custom_call" | custom-call | flops 1557135360 | bytes 6242304 | tf_op jit(solution)/shard_map/dft/pallas_call | solution.py:104
  66.0 1.1 collective-permute-start.16
  67.1 2.4 %collective-permute-done.13.refs_4_ = bf16[48,1408]{1,0:T(8,128)(2,1)S(1)} collective-permute-done((bf16[48,1408]{1,0:T(8,128)(2,1)S(1)}, bf16[48,1408]{1,0:T(8,128)(2,1)S(1)}, u32[]{:S(2)}, u32[]{:S(2)}) %collective-permute-start.13) | collective-permute-done | bytes 135200 | tf_op jit(solution)/shard_map/ppermute | solution.py:290
  69.6 5.8 %collective-permute-done.14.refs_5_ = bf16[48,1408]{1,0:T(8,128)(2,1)S(1)} collective-permute-done((bf16[48,1408]{1,0:T(8,128)(2,1)S(1)}, bf16[48,1408]{1,0:T(8,128)(2,1)S(1)}, u32[]{:S(2)}, u32[]{:S(2)}) %collective-permute-start.14) | collective-permute-done | bytes 135200 | tf_op jit(solution)/shard_map/ppermute | solution.py:290
  75.3 1.4 collective-permute-start.1
  76.8 3.2 %collective-permute-done.15.refs_6_ = bf16[48,1408]{1,0:T(8,128)(2,1)S(1)} collective-permute-done((bf16[48,1408]{1,0:T(8,128)(2,1)S(1)}, bf16[48,1408]{1,0:T(8,128)(2,1)S(1)}, u32[]{:S(2)}, u32[]{:S(2)}) %collective-permute-start.15) | collective-permute-done | bytes 135200 | tf_op jit(solution)/shard_map/ppermute | solution.py:290
  80.0 1.5 collective-permute-start.38
  81.6 2.6 %collective-permute-start.3 = (bf16[48,1408]{1,0:T(8,128)(2,1)}, bf16[48,1408]{1,0:T(8,128)(2,1)S(1)}, u32[]{:S(2)}, u32[]{:S(2)}) collective-permute-start(bf16[48,1408]{1,0:T(8,128)(2,1)} %get-tuple-element.41), channel_id=1, source_target_pairs={{0,16},{4,20},{8,24},{12,28},{16,0},{20,4},{24,8},{28,12},{1,17},{... | collective-permute-start | bytes 405512 | tf_op jit(solution)/shard_map/ppermute | solution.py:290
  84.2 3.0 %collective-permute-done.2.refs_3_ = bf16[48,1408]{1,0:T(8,128)(2,1)S(1)} collective-permute-done((bf16[48,1408]{1,0:T(8,128)(2,1)}, bf16[48,1408]{1,0:T(8,128)(2,1)S(1)}, u32[]{:S(2)}, u32[]{:S(2)}) %collective-permute-start.2) | collective-permute-done | bytes 135200 | tf_op jit(solution)/shard_map/ppermute | solution.py:290
  87.2 1.5 collective-permute-start.5
  88.7 8.5 %collective-permute-done.3.refs_4_ = bf16[48,1408]{1,0:T(8,128)(2,1)S(1)} collective-permute-done((bf16[48,1408]{1,0:T(8,128)(2,1)}, bf16[48,1408]{1,0:T(8,128)(2,1)S(1)}, u32[]{:S(2)}, u32[]{:S(2)}) %collective-permute-start.3) | collective-permute-done | bytes 135200 | tf_op jit(solution)/shard_map/ppermute | solution.py:290
  97.2 7.0 %parity.6.refs_0_ = bf16[24,176,128]{2,1,0:T(8,128)(2,1)} custom-call(s32[1]{0:T(128)} %bitcast.2.me_ref, bf16[48,1408]{1,0:T(8,128)(2,1)} %get-tuple-element.53.refs_0_, bf16[48,1408]{1,0:T(8,128)(2,1)} %copy-done.9, bf16[48,1408]{1,0:T(8,128)(2,1)} %copy-done.10, bf16[48,1408]{1,0:T(8,128)(2,1)} %copy-done.11, bf16[48,1408]{1,0:T(8,128)(2,1)} %copy-done.12, ...), custom_call_target="tpu_custom_call" | custom-call | flops 10813440 | bytes 2162688 | tf_op jit(solution)/shard_map/parity/pallas_call | solution.py:185
  104.3 1.5 collective-permute-start.28
  105.8 7.0 %parity.5.refs_0_ = bf16[24,176,128]{2,1,0:T(8,128)(2,1)} custom-call(s32[1]{0:T(128)} %bitcast.2.me_ref, bf16[48,1408]{1,0:T(8,128)(2,1)} %get-tuple-element.45.refs_0_, bf16[48,1408]{1,0:T(8,128)(2,1)} %copy-done.15, bf16[48,1408]{1,0:T(8,128)(2,1)} %copy-done.17, bf16[48,1408]{1,0:T(8,128)(2,1)} %copy-done.18, bf16[48,1408]{1,0:T(8,128)(2,1)} %copy-done.19, ...), custom_call_target="tpu_custom_call" | custom-call | flops 10813440 | bytes 2162688 | tf_op jit(solution)/shard_map/parity/pallas_call | solution.py:185
  112.8 1.6 collective-permute-start.27
  114.4 0.5 collective-permute-start.17
  115.0 7.0 %parity.4.refs_0_ = bf16[24,176,128]{2,1,0:T(8,128)(2,1)} custom-call(s32[1]{0:T(128)} %bitcast.2.me_ref, bf16[48,1408]{1,0:T(8,128)(2,1)} %get-tuple-element.37.refs_0_, bf16[48,1408]{1,0:T(8,128)(2,1)} %copy-done.22, bf16[48,1408]{1,0:T(8,128)(2,1)} %copy-done.23, bf16[48,1408]{1,0:T(8,128)(2,1)} %copy-done.25, bf16[48,1408]{1,0:T(8,128)(2,1)} %copy-done.26, ...), custom_call_target="tpu_custom_call" | custom-call | flops 10813440 | bytes 2162688 | tf_op jit(solution)/shard_map/parity/pallas_call | solution.py:185
  122.0 0.7 collective-permute-start.8
  122.7 1.4 collective-permute-start.39
  124.1 7.3 %collective-permute-done.28.refs_2_ = bf16[24,176,128]{2,1,0:T(8,128)(2,1)} collective-permute-done((bf16[24,176,128]{2,1,0:T(8,128)(2,1)}, bf16[24,176,128]{2,1,0:T(8,128)(2,1)}, u32[]{:S(2)}, u32[]{:S(2)}) %collective-permute-start.28) | collective-permute-done | bytes 1081376 | tf_op jit(solution)/shard_map/ppermute | solution.py:298
  131.4 1.5 collective-permute-start.29
  132.9 6.6 %collective-permute-done.27.refs_1_ = bf16[24,176,128]{2,1,0:T(8,128)(2,1)S(1)} collective-permute-done((bf16[24,176,128]{2,1,0:T(8,128)(2,1)S(1)}, bf16[24,176,128]{2,1,0:T(8,128)(2,1)S(1)}, u32[]{:S(2)}, u32[]{:S(2)}) %collective-permute-start.27) | collective-permute-done | bytes 1081376 | tf_op jit(solution)/shard_map/ppermute | solution.py:298
  139.5 0.6 collective-permute-start.18
  140.1 0.4 copy-done.3
  140.5 22.3 %collective-permute-done.17.refs_1_ = bf16[24,176,128]{2,1,0:T(8,128)(2,1)} collective-permute-done((bf16[24,176,128]{2,1,0:T(8,128)(2,1)}, bf16[24,176,128]{2,1,0:T(8,128)(2,1)}, u32[]{:S(2)}, u32[]{:S(2)}) %collective-permute-start.17) | collective-permute-done | bytes 1081376 | tf_op jit(solution)/shard_map/ppermute | solution.py:298
  162.8 0.6 collective-permute-start.19
  163.4 1.5 collective-permute-start.7
  164.9 5.0 %collective-permute-done.39.refs_3_ = bf16[16,176,128]{2,1,0:T(8,128)(2,1)S(1)} collective-permute-done((bf16[16,176,128]{2,1,0:T(8,128)(2,1)S(1)}, bf16[16,176,128]{2,1,0:T(8,128)(2,1)S(1)}, u32[]{:S(2)}, u32[]{:S(2)}) %collective-permute-start.39) | collective-permute-done | bytes 720928 | tf_op jit(solution)/shard_map/ppermute | solution.py:298
  170.0 0.9 copy-done.8
  170.8 1.5 collective-permute-start.9
  172.3 0.7 pad_add_fusion.info_ref
  173.0 4.6 %project.4.refs_4_ = f32[88,176,128]{2,1,0:T(8,128)} custom-call(s32[2]{0:T(128)} %pad_add_fusion.info_ref, bf16[88,176,352]{2,1,0:T(8,128)(2,1)} %table_ref.7, bf16[16,176,128]{2,1,0:T(8,128)(2,1)} %parity.7.refs_0_, bf16[16,176,128]{2,1,0:T(8,128)(2,1)} %copy-done.6, bf16[16,176,128]{2,1,0:T(8,128)(2,1)} %copy-done.7, bf16[16,176,128]{2,1,0:T(8,128)(2,1)} %copy-done.8), custom_call_target="tpu_custom_call" | custom-call | flops 507510784 | bytes 6307840 | tf_op jit(solution)/shard_map/project/pallas_call | solution.py:258
  177.6 8.4 %collective-permute-done.29.refs_3_ = bf16[24,176,128]{2,1,0:T(8,128)(2,1)} collective-permute-done((bf16[24,176,128]{2,1,0:T(8,128)(2,1)}, bf16[24,176,128]{2,1,0:T(8,128)(2,1)}, u32[]{:S(2)}, u32[]{:S(2)}) %collective-permute-start.29) | collective-permute-done | bytes 1081376 | tf_op jit(solution)/shard_map/ppermute | solution.py:298
  186.0 6.5 %project.5.refs_4_ = f32[88,176,128]{2,1,0:T(8,128)} custom-call(s32[2]{0:T(128)} %pad_add_fusion.info_ref, bf16[88,176,352]{2,1,0:T(8,128)(2,1)} %table_ref.7, bf16[24,176,128]{2,1,0:T(8,128)(2,1)} %parity.6.refs_0_, bf16[24,176,128]{2,1,0:T(8,128)(2,1)} %copy-done.3, ...), custom_call_target="tpu_custom_call", output_to_operand_aliasing={{}: (6, {})} | custom-call | flops 761266176 | bytes 9461760 | tf_op jit(solution)/shard_map/project/pallas_call | solution.py:258
  192.4 0.7 collective-permute-done.18.refs_2_
  193.1 23.1 %collective-permute-done.19.refs_3_ = bf16[24,176,128]{2,1,0:T(8,128)(2,1)} collective-permute-done((bf16[24,176,128]{2,1,0:T(8,128)(2,1)}, bf16[24,176,128]{2,1,0:T(8,128)(2,1)}, u32[]{:S(2)}, u32[]{:S(2)}) %collective-permute-start.19) | collective-permute-done | bytes 1081376 | tf_op jit(solution)/shard_map/ppermute | solution.py:298
  216.2 6.5 %project.6.refs_4_ = f32[88,176,128]{2,1,0:T(8,128)} custom-call(s32[2]{0:T(128)} %pad_add_fusion.info_ref, bf16[88,176,352]{2,1,0:T(8,128)(2,1)} %table_ref.7, bf16[24,176,128]{2,1,0:T(8,128)(2,1)} %parity.5.refs_0_, bf16[24,176,128]{2,1,0:T(8,128)(2,1)} %collective-permute-done.17.refs_1_, ...), custom_call_target="tpu_custom_call", output_to_operand_aliasing={{}: (6, {})} | custom-call | flops 761266176 | bytes 9461760 | tf_op jit(solution)/shard_map/project/pallas_call | solution.py:258
  222.7 9.4 %collective-permute-done.9.refs_3_ = bf16[24,176,128]{2,1,0:T(8,128)(2,1)} collective-permute-done((bf16[24,176,128]{2,1,0:T(8,128)(2,1)}, bf16[24,176,128]{2,1,0:T(8,128)(2,1)}, u32[]{:S(2)}, u32[]{:S(2)}) %collective-permute-start.9) | collective-permute-done | bytes 1081376 | tf_op jit(solution)/shard_map/ppermute | solution.py:298
  232.1 6.5 %project.7 = f32[88,176,128]{2,1,0:T(8,128)} custom-call(s32[2]{0:T(128)} %pad_add_fusion.info_ref, bf16[88,176,352]{2,1,0:T(8,128)(2,1)} %table_ref.7, bf16[24,176,128]{2,1,0:T(8,128)(2,1)} %parity.4.refs_0_, bf16[24,176,128]{2,1,0:T(8,128)(2,1)} %copy-done.5, bf16[24,176,128]{2,1,0:T(8,128)(2,1)} %collective-permute-done.8.refs_2_, ...), custom_call_target="tpu_custom_call", output_to_operand_aliasing={{}: (6, {})} | custom-call | flops 761266176 | bytes 9461760 | tf_op jit(solution)/shard_map/project/pallas_call | solution.py:258
  (118 shorter events, 0.5 us)
Async XLA Ops:
  11.7 4.5 %collective-permute-start.30 = (bf16[32,1408]{1,0:T(8,128)(2,1)}, bf16[32,1408]{1,0:T(8,128)(2,1)S(1)}, u32[]{:S(2)}, u32[]{:S(2)}) collective-permute-start(bf16[32,1408]{1,0:T(8,128)(2,1)} %get-tuple-element.62), channel_id=1, source_target_pairs={{0,4},{4,0},{8,12},{12,8},{16,20},{20,16},{24,28},{28,24},{1,5},{5... | collective-permute-start | bytes 270344 | tf_op jit(solution)/shard_map/ppermute | solution.py:290
  11.7 6.0 %collective-permute-start.31 = (bf16[32,1408]{1,0:T(8,128)(2,1)}, bf16[32,1408]{1,0:T(8,128)(2,1)S(1)}, u32[]{:S(2)}, u32[]{:S(2)}) collective-permute-start(bf16[32,1408]{1,0:T(8,128)(2,1)} %get-tuple-element.63), channel_id=1, source_target_pairs={{0,8},{4,12},{8,0},{12,4},{16,24},{20,28},{24,16},{28,20},{1,9},{5... | collective-permute-start | bytes 270344 | tf_op jit(solution)/shard_map/ppermute | solution.py:290
  11.7 11.8 %collective-permute-start.32 = (bf16[32,1408]{1,0:T(8,128)(2,1)}, bf16[32,1408]{1,0:T(8,128)(2,1)S(1)}, u32[]{:S(2)}, u32[]{:S(2)}) collective-permute-start(bf16[32,1408]{1,0:T(8,128)(2,1)} %get-tuple-element.64), channel_id=1, source_target_pairs={{0,12},{4,8},{8,4},{12,0},{16,28},{20,24},{24,20},{28,16},{1,13},{... | collective-permute-start | bytes 270344 | tf_op jit(solution)/shard_map/ppermute | solution.py:290
  13.5 13.6 %collective-permute-start.33 = (bf16[32,1408]{1,0:T(8,128)(2,1)}, bf16[32,1408]{1,0:T(8,128)(2,1)S(1)}, u32[]{:S(2)}, u32[]{:S(2)}) collective-permute-start(bf16[32,1408]{1,0:T(8,128)(2,1)} %get-tuple-element.65), channel_id=1, source_target_pairs={{0,16},{4,20},{8,24},{12,28},{16,0},{20,4},{24,8},{28,12},{1,17},{... | collective-permute-start | bytes 270344 | tf_op jit(solution)/shard_map/ppermute | solution.py:290
  16.1 12.9 %collective-permute-start.34 = (bf16[32,1408]{1,0:T(8,128)(2,1)}, bf16[32,1408]{1,0:T(8,128)(2,1)S(1)}, u32[]{:S(2)}, u32[]{:S(2)}) collective-permute-start(bf16[32,1408]{1,0:T(8,128)(2,1)} %get-tuple-element.66), channel_id=1, source_target_pairs={{0,20},{4,16},{8,28},{12,24},{16,4},{20,0},{24,12},{28,8},{1,21},{... | collective-permute-start | bytes 270344 | tf_op jit(solution)/shard_map/ppermute | solution.py:290
  16.1 14.9 %collective-permute-start.35 = (bf16[32,1408]{1,0:T(8,128)(2,1)}, bf16[32,1408]{1,0:T(8,128)(2,1)S(1)}, u32[]{:S(2)}, u32[]{:S(2)}) collective-permute-start(bf16[32,1408]{1,0:T(8,128)(2,1)} %get-tuple-element.67), channel_id=1, source_target_pairs={{0,24},{4,28},{8,16},{12,20},{16,8},{20,12},{24,0},{28,4},{1,25},{... | collective-permute-start | bytes 270344 | tf_op jit(solution)/shard_map/ppermute | solution.py:290
  17.7 14.9 %collective-permute-start.36 = (bf16[32,1408]{1,0:T(8,128)(2,1)}, bf16[32,1408]{1,0:T(8,128)(2,1)S(1)}, u32[]{:S(2)}, u32[]{:S(2)}) collective-permute-start(bf16[32,1408]{1,0:T(8,128)(2,1)} %get-tuple-element.68), channel_id=1, source_target_pairs={{0,28},{4,24},{8,20},{12,16},{16,12},{20,8},{24,4},{28,0},{1,29},{... | collective-permute-start | bytes 270344 | tf_op jit(solution)/shard_map/ppermute | solution.py:290
  23.5 15.1 %copy-start.32 = (bf16[32,1408]{1,0:T(8,128)(2,1)}, bf16[32,1408]{1,0:T(8,128)(2,1)S(1)}, u32[]{:S(2)}) copy-start(bf16[32,1408]{1,0:T(8,128)(2,1)S(1)} %collective-permute-done.32.refs_3_) | copy-start | bytes 270340
  23.5 15.2 %collective-permute-start.20 = (bf16[48,1408]{1,0:T(8,128)(2,1)}, bf16[48,1408]{1,0:T(8,128)(2,1)S(1)}, u32[]{:S(2)}, u32[]{:S(2)}) collective-permute-start(bf16[48,1408]{1,0:T(8,128)(2,1)} %get-tuple-element.54), channel_id=1, source_target_pairs={{0,4},{4,0},{8,12},{12,8},{16,20},{20,16},{24,28},{28,24},{1,5},{5... | collective-permute-start | bytes 405512 | tf_op jit(solution)/shard_map/ppermute | solution.py:290
  27.1 13.2 %collective-permute-start.21 = (bf16[48,1408]{1,0:T(8,128)(2,1)}, bf16[48,1408]{1,0:T(8,128)(2,1)S(1)}, u32[]{:S(2)}, u32[]{:S(2)}) collective-permute-start(bf16[48,1408]{1,0:T(8,128)(2,1)} %get-tuple-element.55), channel_id=1, source_target_pairs={{0,8},{4,12},{8,0},{12,4},{16,24},{20,28},{24,16},{28,20},{1,9},{5... | collective-permute-start | bytes 405512 | tf_op jit(solution)/shard_map/ppermute | solution.py:290
  29.1 12.9 %collective-permute-start.22 = (bf16[48,1408]{1,0:T(8,128)(2,1)}, bf16[48,1408]{1,0:T(8,128)(2,1)S(1)}, u32[]{:S(2)}, u32[]{:S(2)}) collective-permute-start(bf16[48,1408]{1,0:T(8,128)(2,1)} %get-tuple-element.56), channel_id=1, source_target_pairs={{0,12},{4,8},{8,4},{12,0},{16,28},{20,24},{24,20},{28,16},{1,13},{... | collective-permute-start | bytes 405512 | tf_op jit(solution)/shard_map/ppermute | solution.py:290
  31.0 11.1 %collective-permute-start.23 = (bf16[48,1408]{1,0:T(8,128)(2,1)}, bf16[48,1408]{1,0:T(8,128)(2,1)S(1)}, u32[]{:S(2)}, u32[]{:S(2)}) collective-permute-start(bf16[48,1408]{1,0:T(8,128)(2,1)} %get-tuple-element.57), channel_id=1, source_target_pairs={{0,16},{4,20},{8,24},{12,28},{16,0},{20,4},{24,8},{28,12},{1,17},{... | collective-permute-start | bytes 405512 | tf_op jit(solution)/shard_map/ppermute | solution.py:290
  32.5 18.2 %collective-permute-start.24 = (bf16[48,1408]{1,0:T(8,128)(2,1)}, bf16[48,1408]{1,0:T(8,128)(2,1)S(1)}, u32[]{:S(2)}, u32[]{:S(2)}) collective-permute-start(bf16[48,1408]{1,0:T(8,128)(2,1)} %get-tuple-element.58), channel_id=1, source_target_pairs={{0,20},{4,16},{8,28},{12,24},{16,4},{20,0},{24,12},{28,8},{1,21},{... | collective-permute-start | bytes 405512 | tf_op jit(solution)/shard_map/ppermute | solution.py:290
  38.6 15.2 %copy-start.43 = (bf16[48,1408]{1,0:T(8,128)(2,1)S(1)}, bf16[48,1408]{1,0:T(8,128)(2,1)}, u32[]{:S(2)}) copy-start(bf16[48,1408]{1,0:T(8,128)(2,1)} %get-tuple-element.48) | copy-start | bytes 405508
  38.7 18.2 %copy-start.41 = (bf16[48,1408]{1,0:T(8,128)(2,1)S(1)}, bf16[48,1408]{1,0:T(8,128)(2,1)}, u32[]{:S(2)}) copy-start(bf16[48,1408]{1,0:T(8,128)(2,1)} %get-tuple-element.49) | copy-start | bytes 405508
  38.7 18.2 %copy-start.39 = (bf16[48,1408]{1,0:T(8,128)(2,1)S(1)}, bf16[48,1408]{1,0:T(8,128)(2,1)}, u32[]{:S(2)}) copy-start(bf16[48,1408]{1,0:T(8,128)(2,1)} %get-tuple-element.50) | copy-start | bytes 405508
  38.7 20.6 %copy-start.38 = (bf16[48,1408]{1,0:T(8,128)(2,1)S(1)}, bf16[48,1408]{1,0:T(8,128)(2,1)}, u32[]{:S(2)}) copy-start(bf16[48,1408]{1,0:T(8,128)(2,1)} %get-tuple-element.51) | copy-start | bytes 405508
  38.7 27.2 %copy-start.9 = (bf16[48,1408]{1,0:T(8,128)(2,1)}, bf16[48,1408]{1,0:T(8,128)(2,1)S(1)}, u32[]{:S(2)}) copy-start(bf16[48,1408]{1,0:T(8,128)(2,1)S(1)} %collective-permute-done.20.refs_1_) | copy-start | bytes 405508
  38.7 15.2 %collective-permute-start.25 = (bf16[48,1408]{1,0:T(8,128)(2,1)S(1)}, bf16[48,1408]{1,0:T(8,128)(2,1)S(1)}, u32[]{:S(2)}, u32[]{:S(2)}) collective-permute-start(bf16[48,1408]{1,0:T(8,128)(2,1)S(1)} %copy-done.42), channel_id=1, source_target_pairs={{0,24},{4,28},{8,16},{12,20},{16,8},{20,12},{24,0},{28,4},{1,25},{... | collective-permute-start | bytes 405512 | tf_op jit(solution)/shard_map/ppermute | solution.py:290
  40.3 25.6 %copy-start.10 = (bf16[48,1408]{1,0:T(8,128)(2,1)}, bf16[48,1408]{1,0:T(8,128)(2,1)S(1)}, u32[]{:S(2)}) copy-start(bf16[48,1408]{1,0:T(8,128)(2,1)S(1)} %collective-permute-done.21.refs_2_) | copy-start | bytes 405508
  40.3 16.6 %collective-permute-start.26 = (bf16[48,1408]{1,0:T(8,128)(2,1)S(1)}, bf16[48,1408]{1,0:T(8,128)(2,1)S(1)}, u32[]{:S(2)}, u32[]{:S(2)}) collective-permute-start(bf16[48,1408]{1,0:T(8,128)(2,1)S(1)} %copy-done.40), channel_id=1, source_target_pairs={{0,28},{4,24},{8,20},{12,16},{16,12},{20,8},{24,4},{28,0},{1,29},{... | collective-permute-start | bytes 405512 | tf_op jit(solution)/shard_map/ppermute | solution.py:290
  41.9 24.0 %copy-start.11 = (bf16[48,1408]{1,0:T(8,128)(2,1)}, bf16[48,1408]{1,0:T(8,128)(2,1)S(1)}, u32[]{:S(2)}) copy-start(bf16[48,1408]{1,0:T(8,128)(2,1)S(1)} %collective-permute-done.22.refs_3_) | copy-start | bytes 405508
  41.9 15.0 %collective-permute-start.10 = (bf16[48,1408]{1,0:T(8,128)(2,1)}, bf16[48,1408]{1,0:T(8,128)(2,1)S(1)}, u32[]{:S(2)}, u32[]{:S(2)}) collective-permute-start(bf16[48,1408]{1,0:T(8,128)(2,1)} %get-tuple-element.46), channel_id=1, source_target_pairs={{0,4},{4,0},{8,12},{12,8},{16,20},{20,16},{24,28},{28,24},{1,5},{5... | collective-permute-start | bytes 405512 | tf_op jit(solution)/shard_map/ppermute | solution.py:290
  42.1 23.9 %copy-start.12 = (bf16[48,1408]{1,0:T(8,128)(2,1)}, bf16[48,1408]{1,0:T(8,128)(2,1)S(1)}, u32[]{:S(2)}) copy-start(bf16[48,1408]{1,0:T(8,128)(2,1)S(1)} %collective-permute-done.23.refs_4_) | copy-start | bytes 405508
  42.1 17.1 %collective-permute-start.11 = (bf16[48,1408]{1,0:T(8,128)(2,1)}, bf16[48,1408]{1,0:T(8,128)(2,1)S(1)}, u32[]{:S(2)}, u32[]{:S(2)}) collective-permute-start(bf16[48,1408]{1,0:T(8,128)(2,1)} %get-tuple-element.47), channel_id=1, source_target_pairs={{0,8},{4,12},{8,0},{12,4},{16,24},{20,28},{24,16},{28,20},{1,9},{5... | collective-permute-start | bytes 405512 | tf_op jit(solution)/shard_map/ppermute | solution.py:290
  50.7 15.3 %copy-start.13 = (bf16[48,1408]{1,0:T(8,128)(2,1)}, bf16[48,1408]{1,0:T(8,128)(2,1)S(1)}, u32[]{:S(2)}) copy-start(bf16[48,1408]{1,0:T(8,128)(2,1)S(1)} %collective-permute-done.24.refs_5_) | copy-start | bytes 405508
  50.7 71.3 %collective-permute-start.37 = (bf16[16,176,128]{2,1,0:T(8,128)(2,1)}, bf16[16,176,128]{2,1,0:T(8,128)(2,1)S(1)}, u32[]{:S(2)}, u32[]{:S(2)}) collective-permute-start(bf16[16,176,128]{2,1,0:T(8,128)(2,1)} %parity.7.refs_0_), channel_id=1, source_target_pairs={{0,1},{1,0},{2,3},{3,2},{4,5},{5,4},{6,7},{7,6},{8,9},{9,8},{10,11... | collective-permute-start | bytes 2162696 | tf_op jit(solution)/shard_map/ppermute | solution.py:298
  53.9 12.1 %copy-start.14 = (bf16[48,1408]{1,0:T(8,128)(2,1)}, bf16[48,1408]{1,0:T(8,128)(2,1)S(1)}, u32[]{:S(2)}) copy-start(bf16[48,1408]{1,0:T(8,128)(2,1)S(1)} %collective-permute-done.25.refs_6_) | copy-start | bytes 405508
  53.9 12.1 %collective-permute-start.12 = (bf16[48,1408]{1,0:T(8,128)(2,1)S(1)}, bf16[48,1408]{1,0:T(8,128)(2,1)S(1)}, u32[]{:S(2)}, u32[]{:S(2)}) collective-permute-start(bf16[48,1408]{1,0:T(8,128)(2,1)S(1)} %copy-done.43), channel_id=1, source_target_pairs={{0,12},{4,8},{8,4},{12,0},{16,28},{20,24},{24,20},{28,16},{1,13},{... | collective-permute-start | bytes 405512 | tf_op jit(solution)/shard_map/ppermute | solution.py:290
  56.9 12.7 %collective-permute-start.13 = (bf16[48,1408]{1,0:T(8,128)(2,1)S(1)}, bf16[48,1408]{1,0:T(8,128)(2,1)S(1)}, u32[]{:S(2)}, u32[]{:S(2)}) collective-permute-start(bf16[48,1408]{1,0:T(8,128)(2,1)S(1)} %copy-done.41), channel_id=1, source_target_pairs={{0,16},{4,20},{8,24},{12,28},{16,0},{20,4},{24,8},{28,12},{1,17},{... | collective-permute-start | bytes 405512 | tf_op jit(solution)/shard_map/ppermute | solution.py:290
  56.9 18.4 %collective-permute-start.14 = (bf16[48,1408]{1,0:T(8,128)(2,1)S(1)}, bf16[48,1408]{1,0:T(8,128)(2,1)S(1)}, u32[]{:S(2)}, u32[]{:S(2)}) collective-permute-start(bf16[48,1408]{1,0:T(8,128)(2,1)S(1)} %copy-done.39), channel_id=1, source_target_pairs={{0,20},{4,16},{8,28},{12,24},{16,4},{20,0},{24,12},{28,8},{1,21},{... | collective-permute-start | bytes 405512 | tf_op jit(solution)/shard_map/ppermute | solution.py:290
  59.2 20.8 %copy-start.2 = (bf16[16,176,128]{2,1,0:T(8,128)(2,1)S(1)}, bf16[16,176,128]{2,1,0:T(8,128)(2,1)}, u32[]{:S(2)}) copy-start(bf16[16,176,128]{2,1,0:T(8,128)(2,1)} %parity.7.refs_0_) | copy-start | bytes 2162692
  59.2 20.8 %collective-permute-start.15 = (bf16[48,1408]{1,0:T(8,128)(2,1)S(1)}, bf16[48,1408]{1,0:T(8,128)(2,1)S(1)}, u32[]{:S(2)}, u32[]{:S(2)}) collective-permute-start(bf16[48,1408]{1,0:T(8,128)(2,1)S(1)} %copy-done.38), channel_id=1, source_target_pairs={{0,24},{4,28},{8,16},{12,20},{16,8},{20,12},{24,0},{28,4},{1,25},{... | collective-permute-start | bytes 405512 | tf_op jit(solution)/shard_map/ppermute | solution.py:290
  66.0 38.2 %copy-start.18 = (bf16[48,1408]{1,0:T(8,128)(2,1)}, bf16[48,1408]{1,0:T(8,128)(2,1)S(1)}, u32[]{:S(2)}) copy-start(bf16[48,1408]{1,0:T(8,128)(2,1)S(1)} %collective-permute-done.12.refs_3_) | copy-start | bytes 405508
  66.0 15.5 %collective-permute-start.16 = (bf16[48,1408]{1,0:T(8,128)(2,1)S(1)}, bf16[48,1408]{1,0:T(8,128)(2,1)S(1)}, u32[]{:S(2)}, u32[]{:S(2)}) collective-permute-start(bf16[48,1408]{1,0:T(8,128)(2,1)S(1)} %copy-done.37), channel_id=1, source_target_pairs={{0,28},{4,24},{8,20},{12,16},{16,12},{20,8},{24,4},{28,0},{1,29},{... | collective-permute-start | bytes 405512 | tf_op jit(solution)/shard_map/ppermute | solution.py:290
  69.6 34.7 %copy-start.19 = (bf16[48,1408]{1,0:T(8,128)(2,1)}, bf16[48,1408]{1,0:T(8,128)(2,1)S(1)}, u32[]{:S(2)}) copy-start(bf16[48,1408]{1,0:T(8,128)(2,1)S(1)} %collective-permute-done.13.refs_4_) | copy-start | bytes 405508
  69.6 12.0 %collective-permute-start = (bf16[48,1408]{1,0:T(8,128)(2,1)}, bf16[48,1408]{1,0:T(8,128)(2,1)S(1)}, u32[]{:S(2)}, u32[]{:S(2)}) collective-permute-start(bf16[48,1408]{1,0:T(8,128)(2,1)} %get-tuple-element.38), channel_id=1, source_target_pairs={{0,4},{4,0},{8,12},{12,8},{16,20},{20,16},{24,28},{28,24},{1,5},{5... | collective-permute-start | bytes 405512 | tf_op jit(solution)/shard_map/ppermute | solution.py:290
  75.3 28.9 %copy-start.20 = (bf16[48,1408]{1,0:T(8,128)(2,1)}, bf16[48,1408]{1,0:T(8,128)(2,1)S(1)}, u32[]{:S(2)}) copy-start(bf16[48,1408]{1,0:T(8,128)(2,1)S(1)} %collective-permute-done.14.refs_5_) | copy-start | bytes 405508
  75.3 8.9 %collective-permute-start.1 = (bf16[48,1408]{1,0:T(8,128)(2,1)}, bf16[48,1408]{1,0:T(8,128)(2,1)S(1)}, u32[]{:S(2)}, u32[]{:S(2)}) collective-permute-start(bf16[48,1408]{1,0:T(8,128)(2,1)} %get-tuple-element.39), channel_id=1, source_target_pairs={{0,8},{4,12},{8,0},{12,4},{16,24},{20,28},{24,16},{28,20},{1,9},{5... | collective-permute-start | bytes 405512 | tf_op jit(solution)/shard_map/ppermute | solution.py:290
  80.0 24.2 %copy-start.21 = (bf16[48,1408]{1,0:T(8,128)(2,1)}, bf16[48,1408]{1,0:T(8,128)(2,1)S(1)}, u32[]{:S(2)}) copy-start(bf16[48,1408]{1,0:T(8,128)(2,1)S(1)} %collective-permute-done.15.refs_6_) | copy-start | bytes 405508
  80.0 42.7 %collective-permute-start.38 = (bf16[16,176,128]{2,1,0:T(8,128)(2,1)S(1)}, bf16[16,176,128]{2,1,0:T(8,128)(2,1)S(1)}, u32[]{:S(2)}, u32[]{:S(2)}) collective-permute-start(bf16[16,176,128]{2,1,0:T(8,128)(2,1)S(1)} %copy-done.2), channel_id=1, source_target_pairs={{0,2},{1,3},{2,0},{3,1},{4,6},{5,7},{6,4},{7,5},{8,10},{9,11},{10,... | collective-permute-start | bytes 2162696 | tf_op jit(solution)/shard_map/ppermute | solution.py:298
  81.5 22.7 %copy-start.24 = (bf16[48,1408]{1,0:T(8,128)(2,1)}, bf16[48,1408]{1,0:T(8,128)(2,1)S(1)}, u32[]{:S(2)}) copy-start(bf16[48,1408]{1,0:T(8,128)(2,1)S(1)} %collective-permute-done.16.refs_7_) | copy-start | bytes 405508
  81.5 5.7 %collective-permute-start.2 = (bf16[48,1408]{1,0:T(8,128)(2,1)}, bf16[48,1408]{1,0:T(8,128)(2,1)S(1)}, u32[]{:S(2)}, u32[]{:S(2)}) collective-permute-start(bf16[48,1408]{1,0:T(8,128)(2,1)} %get-tuple-element.40), channel_id=1, source_target_pairs={{0,12},{4,8},{8,4},{12,0},{16,28},{20,24},{24,20},{28,16},{1,13},{... | collective-permute-start | bytes 405512 | tf_op jit(solution)/shard_map/ppermute | solution.py:290
  81.6 22.7 %copy-start.22 = (bf16[48,1408]{1,0:T(8,128)(2,1)}, bf16[48,1408]{1,0:T(8,128)(2,1)S(1)}, u32[]{:S(2)}) copy-start(bf16[48,1408]{1,0:T(8,128)(2,1)S(1)} %collective-permute-done.refs_1_) | copy-start | bytes 405508
  81.6 15.7 %collective-permute-start.3 = (bf16[48,1408]{1,0:T(8,128)(2,1)}, bf16[48,1408]{1,0:T(8,128)(2,1)S(1)}, u32[]{:S(2)}, u32[]{:S(2)}) collective-permute-start(bf16[48,1408]{1,0:T(8,128)(2,1)} %get-tuple-element.41), channel_id=1, source_target_pairs={{0,16},{4,20},{8,24},{12,28},{16,0},{20,4},{24,8},{28,12},{1,17},{... | collective-permute-start | bytes 405512 | tf_op jit(solution)/shard_map/ppermute | solution.py:290
  84.2 20.1 %copy-start.23 = (bf16[48,1408]{1,0:T(8,128)(2,1)}, bf16[48,1408]{1,0:T(8,128)(2,1)S(1)}, u32[]{:S(2)}) copy-start(bf16[48,1408]{1,0:T(8,128)(2,1)S(1)} %collective-permute-done.1.refs_2_) | copy-start | bytes 405508
  84.2 20.1 %collective-permute-start.4 = (bf16[48,1408]{1,0:T(8,128)(2,1)}, bf16[48,1408]{1,0:T(8,128)(2,1)S(1)}, u32[]{:S(2)}, u32[]{:S(2)}) collective-permute-start(bf16[48,1408]{1,0:T(8,128)(2,1)} %get-tuple-element.42), channel_id=1, source_target_pairs={{0,20},{4,16},{8,28},{12,24},{16,4},{20,0},{24,12},{28,8},{1,21},{... | collective-permute-start | bytes 405512 | tf_op jit(solution)/shard_map/ppermute | solution.py:290
  87.2 17.1 %copy-start.25 = (bf16[48,1408]{1,0:T(8,128)(2,1)}, bf16[48,1408]{1,0:T(8,128)(2,1)S(1)}, u32[]{:S(2)}) copy-start(bf16[48,1408]{1,0:T(8,128)(2,1)S(1)} %collective-permute-done.2.refs_3_) | copy-start | bytes 405508
  87.2 25.6 %collective-permute-start.5 = (bf16[48,1408]{1,0:T(8,128)(2,1)}, bf16[48,1408]{1,0:T(8,128)(2,1)S(1)}, u32[]{:S(2)}, u32[]{:S(2)}) collective-permute-start(bf16[48,1408]{1,0:T(8,128)(2,1)} %get-tuple-element.43), channel_id=1, source_target_pairs={{0,24},{4,28},{8,16},{12,20},{16,8},{20,12},{24,0},{28,4},{1,25},{... | collective-permute-start | bytes 405512 | tf_op jit(solution)/shard_map/ppermute | solution.py:290
  97.2 17.2 %collective-permute-start.6 = (bf16[48,1408]{1,0:T(8,128)(2,1)}, bf16[48,1408]{1,0:T(8,128)(2,1)S(1)}, u32[]{:S(2)}, u32[]{:S(2)}) collective-permute-start(bf16[48,1408]{1,0:T(8,128)(2,1)} %get-tuple-element.44), channel_id=1, source_target_pairs={{0,28},{4,24},{8,20},{12,16},{16,12},{20,8},{24,4},{28,0},{1,29},{... | collective-permute-start | bytes 405512 | tf_op jit(solution)/shard_map/ppermute | solution.py:290
  104.3 27.1 %collective-permute-start.28 = (bf16[24,176,128]{2,1,0:T(8,128)(2,1)}, bf16[24,176,128]{2,1,0:T(8,128)(2,1)}, u32[]{:S(2)}, u32[]{:S(2)}) collective-permute-start(bf16[24,176,128]{2,1,0:T(8,128)(2,1)} %parity.6.refs_0_), channel_id=1, source_target_pairs={{0,2},{1,3},{2,0},{3,1},{4,6},{5,7},{6,4},{7,5},{8,10},{9,11},{10,... | collective-permute-start | bytes 3244040 | tf_op jit(solution)/shard_map/ppermute | solution.py:298
  112.8 26.7 %collective-permute-start.27 = (bf16[24,176,128]{2,1,0:T(8,128)(2,1)S(1)}, bf16[24,176,128]{2,1,0:T(8,128)(2,1)S(1)}, u32[]{:S(2)}, u32[]{:S(2)}) collective-permute-start(bf16[24,176,128]{2,1,0:T(8,128)(2,1)S(1)} %copy-done), channel_id=1, source_target_pairs={{0,1},{1,0},{2,3},{3,2},{4,5},{5,4},{6,7},{7,6},{8,9},{9,8},{10,11... | collective-permute-start | bytes 3244040 | tf_op jit(solution)/shard_map/ppermute | solution.py:298
  114.4 48.4 %collective-permute-start.17 = (bf16[24,176,128]{2,1,0:T(8,128)(2,1)}, bf16[24,176,128]{2,1,0:T(8,128)(2,1)}, u32[]{:S(2)}, u32[]{:S(2)}) collective-permute-start(bf16[24,176,128]{2,1,0:T(8,128)(2,1)} %parity.5.refs_0_), channel_id=1, source_target_pairs={{0,1},{1,0},{2,3},{3,2},{4,5},{5,4},{6,7},{7,6},{8,9},{9,8},{10,11... | collective-permute-start | bytes 3244040 | tf_op jit(solution)/shard_map/ppermute | solution.py:298
  115.0 24.5 %copy-start.1 = (bf16[24,176,128]{2,1,0:T(8,128)(2,1)S(1)}, bf16[24,176,128]{2,1,0:T(8,128)(2,1)}, u32[]{:S(2)}) copy-start(bf16[24,176,128]{2,1,0:T(8,128)(2,1)} %parity.5.refs_0_) | copy-start | bytes 3244036
  122.0 41.4 %copy-start.6 = (bf16[16,176,128]{2,1,0:T(8,128)(2,1)}, bf16[16,176,128]{2,1,0:T(8,128)(2,1)S(1)}, u32[]{:S(2)}) copy-start(bf16[16,176,128]{2,1,0:T(8,128)(2,1)S(1)} %collective-permute-done.37.refs_1_) | copy-start | bytes 2162692
  122.0 41.4 %collective-permute-start.8 = (bf16[24,176,128]{2,1,0:T(8,128)(2,1)}, bf16[24,176,128]{2,1,0:T(8,128)(2,1)}, u32[]{:S(2)}, u32[]{:S(2)}) collective-permute-start(bf16[24,176,128]{2,1,0:T(8,128)(2,1)} %parity.4.refs_0_), channel_id=1, source_target_pairs={{0,2},{1,3},{2,0},{3,1},{4,6},{5,7},{6,4},{7,5},{8,10},{9,11},{10,... | collective-permute-start | bytes 3244040 | tf_op jit(solution)/shard_map/ppermute | solution.py:298
  122.7 47.3 %copy-start.7 = (bf16[16,176,128]{2,1,0:T(8,128)(2,1)}, bf16[16,176,128]{2,1,0:T(8,128)(2,1)S(1)}, u32[]{:S(2)}) copy-start(bf16[16,176,128]{2,1,0:T(8,128)(2,1)S(1)} %collective-permute-done.38.refs_2_) | copy-start | bytes 2162692
  122.7 47.3 %collective-permute-start.39 = (bf16[16,176,128]{2,1,0:T(8,128)(2,1)S(1)}, bf16[16,176,128]{2,1,0:T(8,128)(2,1)S(1)}, u32[]{:S(2)}, u32[]{:S(2)}) collective-permute-start(bf16[16,176,128]{2,1,0:T(8,128)(2,1)S(1)} %collective-permute-done.37.refs_1_), channel_id=1, source_target_pairs={{0,2},{1,3},{2,0},{3,1},{4,6},{5,7},{6,4},{7,5},{8,10},{9,11},{10,... | collective-permute-start | bytes 2162696 | tf_op jit(solution)/shard_map/ppermute | solution.py:298
  131.4 54.5 %collective-permute-start.29 = (bf16[24,176,128]{2,1,0:T(8,128)(2,1)}, bf16[24,176,128]{2,1,0:T(8,128)(2,1)}, u32[]{:S(2)}, u32[]{:S(2)}) collective-permute-start(bf16[24,176,128]{2,1,0:T(8,128)(2,1)} %collective-permute-done.28.refs_2_), channel_id=1, source_target_pairs={{0,1},{1,0},{2,3},{3,2},{4,5},{5,4},{6,7},{7,6},{8,9},{9,8},{10,11... | collective-permute-start | bytes 3244040 | tf_op jit(solution)/shard_map/ppermute | solution.py:298
  139.5 53.6 %collective-permute-start.18 = (bf16[24,176,128]{2,1,0:T(8,128)(2,1)S(1)}, bf16[24,176,128]{2,1,0:T(8,128)(2,1)S(1)}, u32[]{:S(2)}, u32[]{:S(2)}) collective-permute-start(bf16[24,176,128]{2,1,0:T(8,128)(2,1)S(1)} %copy-done.1), channel_id=1, source_target_pairs={{0,2},{1,3},{2,0},{3,1},{4,6},{5,7},{6,4},{7,5},{8,10},{9,11},{10,... | collective-permute-start | bytes 3244040 | tf_op jit(solution)/shard_map/ppermute | solution.py:298
  162.8 53.4 %collective-permute-start.19 = (bf16[24,176,128]{2,1,0:T(8,128)(2,1)}, bf16[24,176,128]{2,1,0:T(8,128)(2,1)}, u32[]{:S(2)}, u32[]{:S(2)}) collective-permute-start(bf16[24,176,128]{2,1,0:T(8,128)(2,1)} %collective-permute-done.17.refs_1_), channel_id=1, source_target_pairs={{0,2},{1,3},{2,0},{3,1},{4,6},{5,7},{6,4},{7,5},{8,10},{9,11},{10,... | collective-permute-start | bytes 3244040 | tf_op jit(solution)/shard_map/ppermute | solution.py:298
  163.4 59.3 %collective-permute-start.7 = (bf16[24,176,128]{2,1,0:T(8,128)(2,1)}, bf16[24,176,128]{2,1,0:T(8,128)(2,1)S(1)}, u32[]{:S(2)}, u32[]{:S(2)}) collective-permute-start(bf16[24,176,128]{2,1,0:T(8,128)(2,1)} %parity.4.refs_0_), channel_id=1, source_target_pairs={{0,1},{1,0},{2,3},{3,2},{4,5},{5,4},{6,7},{7,6},{8,9},{9,8},{10,11... | collective-permute-start | bytes 3244040 | tf_op jit(solution)/shard_map/ppermute | solution.py:298
  170.8 61.2 %collective-permute-start.9 = (bf16[24,176,128]{2,1,0:T(8,128)(2,1)}, bf16[24,176,128]{2,1,0:T(8,128)(2,1)}, u32[]{:S(2)}, u32[]{:S(2)}) collective-permute-start(bf16[24,176,128]{2,1,0:T(8,128)(2,1)} %collective-permute-done.8.refs_2_), channel_id=1, source_target_pairs={{0,1},{1,0},{2,3},{3,2},{4,5},{5,4},{6,7},{7,6},{8,9},{9,8},{10,11... | collective-permute-start | bytes 3244040 | tf_op jit(solution)/shard_map/ppermute | solution.py:298
  193.1 23.1 %copy-start.4 = (bf16[24,176,128]{2,1,0:T(8,128)(2,1)}, bf16[24,176,128]{2,1,0:T(8,128)(2,1)S(1)}, u32[]{:S(2)}) copy-start(bf16[24,176,128]{2,1,0:T(8,128)(2,1)S(1)} %collective-permute-done.18.refs_2_) | copy-start | bytes 3244036
  (20 other events, 130.2 us)
